TPU v7x, 32 devices: a whole 2x2x4 slice. The times are simulated.
32 devices in a mesh: mem: 8 (over z, core), space: 4 (over y, x).
Axes of the slice: x: 2, y: 2, z: 4, core: 2. Of those that a mesh axis runs over, the one named last changes fastest.
Arguments:
- yb_pert: bfloat16 [256, 16384], P('mem', 'space'), may hold values from -2.5 to 2.5
- innov: float32 [16384], P('space'), may hold values from -6 to 6
- obs_rinv: float32 [16384], P('space'), may hold values from 0.5 to 4
- obs_count: int32 [128], P('space'), may hold values from 32 to 128
- block_list: int32 [32, 4, 16], P('mem', 'space'), may hold values from -1 to 95, as said below
- loc_weight: float32 [32, 4, 16], P('mem', 'space'), may hold values from 0.1 to 1
- state: bfloat16 [256, 4, 32, 576], P('mem', 'space'), may hold values from -6 to 6
Outputs:
- analysis: bfloat16 [256, 4, 32, 576], P('mem', 'space')
Inputs may be any that keep to these rules, and one draw needn't show every extreme that they name: `block_list`: each patch lists distinct blocks of its window, filled slots first then -1; a patch of the first strip lists no block of the previous strip, one of the last strip none of the next; every patch fills at least 8 slots and some patch all 16.
All inputs are finite; a program needn't handle non-finite values.
Results may differ from a plain program's by a relative error of at most 0.012.
Values may be sent and summed in bfloat16 or wider, within the bound.
A program may use at most 64 MiB of HBM per device.

v0:
```python
import jax
import jax.numpy as jnp
from jax import lax
from jax.sharding import PartitionSpec as P

BLOCK = 128
NSI = 6


inflation = 1.1


def extended(cells, sides, width):
    for axis, dim in sides:
        count = lax.axis_size(axis)
        ends = count - 1
        head = lax.slice_in_dim(cells, 0, width, axis=dim)
        tail = lax.slice_in_dim(cells, cells.shape[dim] - width, cells.shape[dim], axis=dim)
        cells = jnp.concatenate(
            [
                lax.ppermute(tail, axis, [(i, (i + 1) % count) for i in range(ends)]),
                cells,
                lax.ppermute(head, axis, [((i + 1) % count, i) for i in range(ends)]),
            ],
            axis=dim,
        )
    return cells


def matmul_high(left, right):
    return jnp.matmul(left, right, precision=lax.Precision.HIGHEST)


def patch_weights(member_win, rinv_win, innov_win, slot_index, slot_loc):
    members = member_win.shape[0]
    patches = slot_index.shape[0]
    slot_clip = jnp.maximum(slot_index, 0)
    slot_live = (slot_index >= 0).astype(jnp.float32)
    chosen = member_win[:, slot_clip, :]
    chosen = jnp.transpose(chosen, (1, 0, 2, 3)).reshape(patches, members, -1)
    weight_obs = rinv_win[slot_clip] * (slot_loc * slot_live)[:, :, None]
    innov_obs = innov_win[slot_clip]
    root_weight = jnp.sqrt(weight_obs).reshape(patches, -1)
    scaled = (chosen.astype(jnp.float32) * root_weight[:, None, :]).astype(jnp.bfloat16)
    gram_matrix = jnp.einsum("pko,pjo->pkj", scaled, scaled, preferred_element_type=jnp.float32)
    projected = jnp.einsum(
        "pko,po->pk",
        scaled.astype(jnp.float32),
        root_weight * innov_obs.reshape(patches, -1),
        precision=lax.Precision.HIGHEST,
    )
    identity = jnp.eye(members, dtype=jnp.float32)
    system = gram_matrix + (members - 1) / inflation * identity
    frob_norm = jnp.sqrt(jnp.sum(system * system, axis=(1, 2)))
    approx_root = system / frob_norm[:, None, None]
    inverse_root = jnp.broadcast_to(identity, system.shape)
    for iteration in range(NSI):
        correction = 1.5 * identity - 0.5 * matmul_high(inverse_root, approx_root)
        approx_root = matmul_high(approx_root, correction)
        inverse_root = matmul_high(correction, inverse_root)
    inv_half = inverse_root / jnp.sqrt(frob_norm)[:, None, None]
    inner = matmul_high(inv_half, projected[:, :, None])
    mean_weight = matmul_high(inv_half, inner)[:, :, 0]
    return (jnp.sqrt(float(members - 1)) * inv_half + mean_weight[:, :, None]).astype(jnp.bfloat16)


def apply_weights(columns, weights):
    state_f32 = columns.astype(jnp.float32)
    ens_mean = jnp.mean(state_f32, axis=0)
    deviation = (state_f32 - ens_mean[None]).astype(jnp.bfloat16)
    analysed = jnp.einsum("jpc,pji->ipc", deviation, weights, preferred_element_type=jnp.float32)
    return (analysed + ens_mean[None]).astype(jnp.bfloat16)


def per_device(yb_pert, innov, obs_rinv, obs_count, block_list, loc_weight, state):
    blocks_here = obs_count.shape[0]
    obs_valid = (jnp.arange(BLOCK, dtype=jnp.int32)[None, :] < obs_count[:, None]).astype(
        jnp.float32
    )
    weighted = (obs_rinv.reshape(blocks_here, BLOCK) * obs_valid).reshape(-1)
    paired = jnp.stack([innov, weighted])
    beside_all = extended(paired.astype(jnp.bfloat16), (("space", 1),), innov.shape[0]).astype(
        paired.dtype
    )
    innov_win = beside_all[0].reshape(-1, BLOCK)
    rinv_win = beside_all[1].reshape(-1, BLOCK)
    rimmed = extended(yb_pert, (("space", 1),), yb_pert.shape[1])
    window = lax.all_gather(rimmed, "mem", axis=0, tiled=True)
    member_win = window.reshape(window.shape[0], -1, BLOCK)
    weights = patch_weights(
        member_win, rinv_win, innov_win, block_list[:, 0, :], loc_weight[:, 0, :]
    )
    columns = lax.all_to_all(state, "mem", split_axis=2, concat_axis=0, tiled=True)
    analysed = apply_weights(columns[:, 0], weights)
    return lax.all_to_all(analysed[:, None], "mem", split_axis=0, concat_axis=2, tiled=True)


def solution(mesh):
    in_specs = (
        P("mem", "space"),
        P("space"),
        P("space"),
        P("space"),
        P("mem", "space", None),
        P("mem", "space", None),
        P("mem", "space", None, None),
    )
    out_specs = P("mem", "space", None, None)
    return jax.shard_map(
        per_device, mesh=mesh, in_specs=in_specs, out_specs=out_specs, check_vma=False
    )
```

profile of v0, /device:TPU:0, one launch (start us, length us, event | category | flops | bytes accessed | tf_op | source)
XLA Modules:
  0.0 219.3 jit_solution(3391781337139638232)
XLA Ops:
  6.5 5.0 %collective-permute-start = (bf16[32,4096]{1,0:T(8,128)(2,1)}, bf16[32,4096]{1,0:T(8,128)(2,1)S(1)}, u32[]{:S(2)}, u32[]{:S(2)}) collective-permute-start(bf16[32,4096]{1,0:T(8,128)(2,1)} %param.7), channel_id=1, source_target_pairs={{0,1},{1,2},{2,3},{4,5},{5,6},{6,7},{8,9},{9,10},{10,11},{12,13},{... | collective-permute-start | bytes 786440 | tf_op jit(solution)/shard_map/ppermute | solution.py:21
  11.5 1.3 collective-permute-start.1
  12.8 4.5 %collective-permute-done = bf16[32,4096]{1,0:T(8,128)(2,1)S(1)} collective-permute-done((bf16[32,4096]{1,0:T(8,128)(2,1)}, bf16[32,4096]{1,0:T(8,128)(2,1)S(1)}, u32[]{:S(2)}, u32[]{:S(2)}) %collective-permute-start) | collective-permute-done | bytes 262176 | tf_op jit(solution)/shard_map/ppermute | solution.py:21
  17.4 7.5 %collective-permute-done.1 = bf16[32,4096]{1,0:T(8,128)(2,1)S(1)} collective-permute-done((bf16[32,4096]{1,0:T(8,128)(2,1)}, bf16[32,4096]{1,0:T(8,128)(2,1)S(1)}, u32[]{:S(2)}, u32[]{:S(2)}) %collective-permute-start.1) | collective-permute-done | bytes 262176 | tf_op jit(solution)/shard_map/ppermute | solution.py:23
  24.8 1.9 pad_maximum_fusion
  26.7 0.8 select_convert_fusion
  27.5 0.7 convert.13
  28.4 3.4 %collective-permute-start.2 = (bf16[2,4096]{1,0:T(2,128)(2,1)S(1)}, bf16[2,4096]{1,0:T(2,128)(2,1)S(1)}, u32[]{:S(2)}, u32[]{:S(2)}) collective-permute-start(bf16[2,4096]{1,0:T(2,128)(2,1)S(1)} %pad_maximum_fusion.1), channel_id=1, source_target_pairs={{0,1},{1,2},{2,3},{4,5},{5,6},{6,7},{8,9},{9,10},{10,11},{12,13},{... | collective-permute-start | bytes 49160 | tf_op jit(solution)/shard_map/ppermute | solution.py:21
  31.8 1.3 collective-permute-start.3
  33.1 1.5 copy.71
  34.5 4.9 %all-to-all-start = ((bf16[32,1,32,576]{3,0,1,2:T(8,128)(2,1)}), bf16[32,1,32,576]{3,0,1,2:T(8,128)(2,1)S(1)}, u32[]{:S(2)}, u32[]{:S(2)}) async-start(bf16[32,1,32,576]{3,0,1,2:T(8,128)(2,1)} %copy.71), calls=%async_computation | async-start | bytes 2621440 | tf_op jit(solution)/shard_map/all_to_all | solution.py:93
  39.8 0.6 gather_fusion.1
  40.5 0.6 gather_fusion.2
  41.2 65.8 %all-to-all-done = bf16[32,1,32,576]{3,0,1,2:T(8,128)(2,1)S(1)} async-done(((bf16[32,1,32,576]{3,0,1,2:T(8,128)(2,1)}), bf16[32,1,32,576]{3,0,1,2:T(8,128)(2,1)S(1)}, u32[]{:S(2)}, u32[]{:S(2)}) %all-to-all-start) | async-done | bytes 1179680 | tf_op jit(solution)/shard_map/all_to_all | solution.py:93
  107.0 0.3 bitcast_convert_fusion
  107.3 1.7 copy.73
  108.9 0.3 fusion.12
  109.3 10.2 %all-gather.2.cloned.1.call-done = bf16[256,12288]{1,0:T(8,128)(2,1)} async-done(((bf16[32,12288]{1,0:T(8,128)(2,1)}), bf16[256,12288]{1,0:T(8,128)(2,1)}) %all-gather.2.cloned.1.call-update) | async-done | bytes 6291472 | tf_op jit(solution)/shard_map/all_gather | solution.py:88
  119.6 8.6 %copy.68 = bf16[256,12288]{0,1:T(8,128)(2,1)} copy(bf16[256,12288]{1,0:T(8,128)(2,1)} %all-gather.2.cloned.1.call-done) | data formatting | bytes 12582912 | tf_op jit(solution)/shard_map/all_gather | solution.py:88
  128.2 8.6 %copy.69 = bf16[256,96,128]{2,0,1:T(8,128)(2,1)} copy(bf16[256,96,128]{0,2,1:T(8,128)(2,1)} %bitcast.94) | data formatting | bytes 12582912 | tf_op jit(solution)/shard_map/reshape | solution.py:89
  136.8 5.9 %gather_fusion = bf16[64,256,128]{2,1,0:T(8,128)(2,1)} fusion(bf16[256,96,128]{2,0,1:T(8,128)(2,1)} %copy.69, s32[1024]{0:T(1024)S(1)} %pad_clamp_fusion), kind=kCustom, calls=%fused_computation | custom fusion | bytes 8388864 | tf_op jit(solution)/shard_map/gather | solution.py:39
  142.7 5.1 %multiply_reduce_fusion = (f32[4]{0:T(128)S(1)}, f32[4,256,256]{2,1,0:T(8,128)S(1)}) fusion(f32[256,256]{1,0:T(8,128)S(1)} %fusion.18, f32[4,2048]{1,0:T(4,128)S(1)} %bitcast.104, bf16[4,16,256,128]{3,2,1,0:T(8,128)(2,1)} %bitcast.99), kind=kOutput, calls=%fused_computation.27 | convolution fusion | flops 1080819712 | bytes 5537808 | tf_op jit(solution)/shard_map/pko,pjo->pkj/dot_general | solution.py:45
  147.9 1.2 fusion.7
  149.0 1.2 fusion.21
  150.2 1.1 fusion.15
  151.3 1.2 fusion.6
  152.5 1.1 fusion.31
  153.7 1.1 fusion.30
  154.8 1.2 fusion.5
  156.0 1.1 fusion.33
  157.2 1.4 fusion.32
  158.6 1.2 fusion.4
  159.8 1.1 fusion.35
  160.9 1.1 fusion.34
  162.1 1.2 fusion.3
  163.3 1.1 fusion.37
  164.4 1.1 fusion.36
  165.6 3.3 %fusion.9 = f32[4,1,256]{2,1,0:T(1,128)S(1)} fusion(f32[4,2048]{1,0:T(4,128)S(1)} %bitcast.105, f32[4,2048,1]{1,0,2:T(4,128)S(1)} %multiply_bitcast_fusion, bf16[4,16,256,128]{3,2,1,0:T(8,128)(2,1)S(1)} %bitcast.100), kind=kOutput, calls=%fused_computation.25 | convolution fusion | flops 31457280 | bytes 4263936 | tf_op jit(solution)/shard_map/pko,po->pk/dot_general | solution.py:46
  168.9 1.2 fusion.2
  170.1 1.4 convolution_divide_fusion
  171.6 1.0 fusion.26
  172.6 1.0 fusion.24
  173.6 1.0 fusion.1
  174.6 1.4 copy.76
  176.0 34.6 %all_to_all.27 = bf16[256,1,4,576]{3,2,1,0:T(4,128)(2,1)S(1)} all-to-all(bf16[256,1,4,576]{3,2,1,0:T(4,128)(2,1)S(1)} %copy.76), channel_id=1, replica_groups=mesh['mem'=8,'space'=4] {'mem'}, dimensions={0} | all-to-all | bytes 2359296 | tf_op jit(solution)/shard_map/all_to_all | solution.py:95
  210.7 0.2 copy.77
  210.8 0.2 copy.78
  211.0 1.5 copy.79
  (37 shorter events, 0.7 us)
Async XLA Ops:
  6.5 26.5 %copy-start.2 = (bf16[32,1,32,576]{3,2,1,0:T(8,128)(2,1)S(1)}, bf16[32,1,32,576]{3,2,1,0:T(8,128)(2,1)}, u32[]{:S(2)}) copy-start(bf16[32,1,32,576]{3,2,1,0:T(8,128)(2,1)} %param.13) | copy-start | bytes 3538948
  6.5 113.1 %all-gather.2.cloned.1.call-start = ((), (), s32[]{:S(2)}) async-start(), calls=%async_computation.2 | async-start | bytes 7077888 | tf_op jit(solution)/shard_map/all_gather | solution.py:88
  6.5 10.8 %collective-permute-start = (bf16[32,4096]{1,0:T(8,128)(2,1)}, bf16[32,4096]{1,0:T(8,128)(2,1)S(1)}, u32[]{:S(2)}, u32[]{:S(2)}) collective-permute-start(bf16[32,4096]{1,0:T(8,128)(2,1)} %param.7), channel_id=1, source_target_pairs={{0,1},{1,2},{2,3},{4,5},{5,6},{6,7},{8,9},{9,10},{10,11},{12,13},{... | collective-permute-start | bytes 786440 | tf_op jit(solution)/shard_map/ppermute | solution.py:21
  11.5 13.3 %collective-permute-start.1 = (bf16[32,4096]{1,0:T(8,128)(2,1)}, bf16[32,4096]{1,0:T(8,128)(2,1)S(1)}, u32[]{:S(2)}, u32[]{:S(2)}) collective-permute-start(bf16[32,4096]{1,0:T(8,128)(2,1)} %param.7), channel_id=1, source_target_pairs={{1,0},{2,1},{3,2},{5,4},{6,5},{7,6},{9,8},{10,9},{11,10},{13,12},{... | collective-permute-start | bytes 786440 | tf_op jit(solution)/shard_map/ppermute | solution.py:23
  28.3 11.1 %copy-start.3 = (s32[4,1,16]{2,1,0:T(1,128)S(1)}, s32[4,1,16]{2,1,0:T(1,128)}, u32[]{:S(2)}) copy-start(s32[4,1,16]{2,1,0:T(1,128)} %param.11) | copy-start | bytes 772
  28.3 11.3 %copy-start.4 = (f32[4,1,16]{2,1,0:T(1,128)S(1)}, f32[4,1,16]{2,1,0:T(1,128)}, u32[]{:S(2)}) copy-start(f32[4,1,16]{2,1,0:T(1,128)} %param.12) | copy-start | bytes 772
  28.4 11.3 %collective-permute-start.2 = (bf16[2,4096]{1,0:T(2,128)(2,1)S(1)}, bf16[2,4096]{1,0:T(2,128)(2,1)S(1)}, u32[]{:S(2)}, u32[]{:S(2)}) collective-permute-start(bf16[2,4096]{1,0:T(2,128)(2,1)S(1)} %pad_maximum_fusion.1), channel_id=1, source_target_pairs={{0,1},{1,2},{2,3},{4,5},{5,6},{6,7},{8,9},{9,10},{10,11},{12,13},{... | collective-permute-start | bytes 49160 | tf_op jit(solution)/shard_map/ppermute | solution.py:21
  31.8 7.9 %collective-permute-start.3 = (bf16[2,4096]{1,0:T(2,128)(2,1)S(1)}, bf16[2,4096]{1,0:T(2,128)(2,1)S(1)}, u32[]{:S(2)}, u32[]{:S(2)}) collective-permute-start(bf16[2,4096]{1,0:T(2,128)(2,1)S(1)} %pad_maximum_fusion.1), channel_id=1, source_target_pairs={{1,0},{2,1},{3,2},{5,4},{6,5},{7,6},{9,8},{10,9},{11,10},{13,12},{... | collective-permute-start | bytes 49160 | tf_op jit(solution)/shard_map/ppermute | solution.py:23
  34.5 72.4 %all-to-all-start = ((bf16[32,1,32,576]{3,0,1,2:T(8,128)(2,1)}), bf16[32,1,32,576]{3,0,1,2:T(8,128)(2,1)S(1)}, u32[]{:S(2)}, u32[]{:S(2)}) async-start(bf16[32,1,32,576]{3,0,1,2:T(8,128)(2,1)} %copy.71), calls=%async_computation | async-start | bytes 2621440 | tf_op jit(solution)/shard_map/all_to_all | solution.py:93
  163.3 2.3 %copy-start.1 = (bf16[64,256,128]{2,1,0:T(8,128)(2,1)S(1)}, bf16[64,256,128]{2,1,0:T(8,128)(2,1)}, u32[]{:S(2)}) copy-start(bf16[64,256,128]{2,1,0:T(8,128)(2,1)} %gather_fusion) | copy-start | bytes 12582916
  170.1 3.4 %copy-start = (f32[8,32,1,4,576]{4,1,0,3,2:T(8,128)S(1)}, f32[8,32,1,4,576]{4,1,0,3,2:T(8,128)}, u32[]{:S(2)}) copy-start(f32[8,32,1,4,576]{4,1,0,3,2:T(8,128)} %copy.73) | copy-start | bytes 7077892
Sparse Core Ops, SparseCore 0:
  26.9 92.6 all-gather.1
where the time goes:
time: 220 us; the launch traced here: 219 us
  waiting for transfers between devices  88.1 us (40%)
  blocking collectives  34.6 us (16%)
  matrix products  31.7 us (14%)
  local copies, waits for them, and re-layouts  30.9 us (14%)
  starting transfers between devices  15.8 us (7%)
  between operations  13.8 us (6%)
  other arithmetic  4.36 us (2%)
    all_to_all x1, waiting for transfers between devices, per_device(): lax.all_to_all(state, 'mem', split_axis=2, concat_axis=0, tiled=True)  65.8 us
    all_to_all x1, blocking collectives, per_device(): lax.all_to_all(analysed[:, None], 'mem', split_axis=0, concat_axis=2, til...  34.6 us
    dot_general x19, matrix products, matmul_high(): return jnp.matmul(left, right, precision=lax.Precision.HIGHEST)  22.2 us
    all_gather x1, waiting for transfers between devices, per_device(): window = lax.all_gather(rimmed, 'mem', axis=0, tiled=True)  10.2 us
    all_gather x1, local copies, waits for them, and re-layouts, per_device(): window = lax.all_gather(rimmed, 'mem', axis=0, tiled=True)  8.62 us
    reshape x1, local copies, waits for them, and re-layouts, per_device(): member_win = window.reshape(window.shape[0], -1, BLOCK)  8.61 us
    ppermute x2, starting transfers between devices, extended(): lax.ppermute(tail, axis, [(i, (i + 1) % count) for i in range(ends)])  8.37 us
    ppermute x2, waiting for transfers between devices, extended(): lax.ppermute(head, axis, [((i + 1) % count, i) for i in range(ends)])  7.46 us
  transfers between devices with their start and end apart: 6, of which 4 were waited for; matrix products, arithmetic and copies ran while one was open for 3% of the time, Pallas kernels for 0%

commit v1 on v0

v1 whole, which is shorter than its diff:
```python
import functools

import jax
import jax.numpy as jnp
from jax import lax
from jax.experimental import pallas as pl
from jax.experimental.pallas import tpu as pltpu
from jax.sharding import PartitionSpec as P

BLOCK = 128
NSI = 6
MESH = pl.DeviceIdType.MESH


inflation = 1.1


def gather_window(nm, ns, yb_ref, aux_ref, win_ref, auxw_ref, local_sem, local_aux_sem,
                  sz, rz, sx, rx, sc, rc, sa, ra):
    mem = lax.axis_index("mem")
    strip = lax.axis_index("space")
    nz = nm // 2
    z, core = mem // 2, lax.rem(mem, 2)
    other = mem + 1 - 2 * core
    width = yb_ref.shape[1]

    def place(index, slot):
        return win_ref.at[index, :, pl.ds(slot * width, width)]

    def peer(step):
        return lax.rem(z + step, nz) * 2 + core

    has = (strip > 0, strip < ns - 1)
    beside = (strip - 1, strip + 1)

    barrier = pltpu.get_barrier_semaphore()
    for step in range(1, nz):
        pl.semaphore_signal(barrier, inc=1, device_id=(peer(step), strip), device_id_type=MESH)
    pl.semaphore_signal(barrier, inc=1, device_id=(other, strip), device_id_type=MESH)
    for side in range(2):
        @pl.when(has[side])
        def _():
            pl.semaphore_signal(barrier, inc=1, device_id=(mem, beside[side]), device_id_type=MESH)
    pl.semaphore_wait(barrier, nz + has[0].astype(jnp.int32) + has[1].astype(jnp.int32))

    keep = pltpu.make_async_copy(yb_ref, place(mem, 1), local_sem)
    keep_aux = pltpu.make_async_copy(aux_ref, auxw_ref.at[1], local_aux_sem)

    def along(step):
        return pltpu.make_async_remote_copy(
            yb_ref, place(mem, 1), sz.at[step], rz.at[step],
            device_id=(peer(step), strip), device_id_type=MESH)

    def across(step, side):
        index = peer(step)
        return pltpu.make_async_remote_copy(
            yb_ref if step == 0 else place(index, 1), place(index, 2 - 2 * side),
            sx.at[side, step], rx.at[side, step],
            device_id=(mem, beside[side]), device_id_type=MESH)

    def arrive(step, side):
        index = peer(step)
        spot = place(index, 2 * side)
        return pltpu.make_async_remote_copy(
            spot, spot, sx.at[1 - side, step], rx.at[1 - side, step],
            device_id=(mem, beside[side]), device_id_type=MESH)

    def arrive_along(step):
        spot = place(peer(nz - step), 1)
        return pltpu.make_async_remote_copy(
            spot, spot, sz.at[step], rz.at[step],
            device_id=(peer(nz - step), strip), device_id_type=MESH)

    def over(step, slot):
        index = peer(step)
        return pltpu.make_async_remote_copy(
            yb_ref if step == 0 and slot == 1 else place(index, slot), place(index, slot),
            sc.at[slot, step], rc.at[slot, step],
            device_id=(other, strip), device_id_type=MESH)

    def arrive_over(step, slot):
        spot = place(lax.rem(z + step, nz) * 2 + 1 - core, slot)
        return pltpu.make_async_remote_copy(
            spot, spot, sc.at[slot, step], rc.at[slot, step],
            device_id=(other, strip), device_id_type=MESH)

    def beside_aux(side):
        return pltpu.make_async_remote_copy(
            aux_ref, auxw_ref.at[2 - 2 * side], sa.at[side], ra.at[side],
            device_id=(mem, beside[side]), device_id_type=MESH)

    def arrive_aux(side):
        return pltpu.make_async_remote_copy(
            aux_ref, auxw_ref.at[2 * side], sa.at[1 - side], ra.at[1 - side],
            device_id=(mem, beside[side]), device_id_type=MESH)

    def send_across(step):
        for side in range(2):
            @pl.when(has[side])
            def _():
                across(step, side).start()

    for step in range(1, nz):
        along(step).start()
    send_across(0)
    keep.start()
    keep_aux.start()
    over(0, 1).start()
    for side in range(2):
        @pl.when(has[side])
        def _():
            beside_aux(side).start()
    order = [nz - step for step in range(1, nz)]
    for step in range(1, nz):
        arrive_along(step).wait_recv()
        send_across(nz - step)
        over(nz - step, 1).start()
    for step in [0] + order:
        for side in range(2):
            @pl.when(has[side])
            def _():
                arrive(step, side).wait_recv()
                over(step, 2 * side).start()
    keep.wait()
    keep_aux.wait()
    for step in range(1, nz):
        along(step).wait_send()
    for step in [0] + order:
        over(step, 1).wait_send()
        arrive_over(step, 1).wait_recv()
        for side in range(2):
            @pl.when(has[side])
            def _():
                across(step, side).wait_send()
                over(step, 2 * side).wait_send()
                arrive_over(step, 2 * side).wait_recv()
    for side in range(2):
        @pl.when(has[side])
        def _():
            beside_aux(side).wait_send()
            arrive_aux(side).wait_recv()


def split(value):
    high = value.astype(jnp.bfloat16)
    return high, (value - high.astype(jnp.float32)).astype(jnp.bfloat16)


def matmul_split(left, right):
    (lh, ll), (rh, rl) = left, right
    return jnp.dot(jnp.concatenate([lh, lh, ll], axis=1),
                   jnp.concatenate([rh, rl, rh], axis=0),
                   preferred_element_type=jnp.float32)


def analyse(blocks, list_ref, loc_ref, win_ref, aux_ref, col_ref, out_ref, scaled_ref):
    nm, patches, rows, cells = col_ref.shape
    members = nm * rows
    slots = list_ref.shape[1]
    identity = (lax.broadcasted_iota(jnp.int32, (members, members), 0)
                == lax.broadcasted_iota(jnp.int32, (members, members), 1)).astype(jnp.float32)
    systems, projected = [], []
    for p in range(patches):
        def slot_body(j, acc):
            q = list_ref[p, j]
            live = (q >= 0).astype(jnp.float32)
            q = jnp.where(q >= 0, q, blocks)
            strip, block = q // blocks, lax.rem(q, blocks)
            lanes = pl.ds(pl.multiple_of(q * BLOCK, BLOCK), BLOCK)
            inner = pl.ds(pl.multiple_of(block * BLOCK, BLOCK), BLOCK)
            aux = aux_ref[strip, :, inner]
            root = jnp.sqrt(aux[1:2, :] * (loc_ref[p, j] * live))
            chunk = win_ref[:, :, lanes].astype(jnp.float32).reshape(members, BLOCK)
            scaled = (chunk * root).astype(jnp.bfloat16)
            scaled_ref[p, :, pl.ds(pl.multiple_of(j * BLOCK, BLOCK), BLOCK)] = scaled
            return acc + scaled.astype(jnp.float32) * (root * aux[0:1, :])
        acc = lax.fori_loop(0, slots, slot_body, jnp.zeros((members, BLOCK), jnp.float32),
                            unroll=4)
        projected.append(jnp.sum(acc, axis=1, keepdims=True))
        scaled = scaled_ref[p]
        gram = lax.dot_general(scaled, scaled, (((1,), (1,)), ((), ())),
                               preferred_element_type=jnp.float32)
        systems.append(gram + (members - 1) / inflation * identity)
    frob = [jnp.sqrt(jnp.sum(s * s, keepdims=True)) for s in systems]
    roots = [s / f for s, f in zip(systems, frob)]
    inverse = [None] * patches
    for iteration in range(NSI):
        for p in range(patches):
            y = split(roots[p])
            if iteration == 0:
                correction = 1.5 * identity - 0.5 * roots[p]
                c = split(correction)
                inverse[p] = correction
            else:
                v = split(inverse[p])
                correction = 1.5 * identity - 0.5 * matmul_split(v, y)
                c = split(correction)
                inverse[p] = matmul_split(c, v)
            if iteration < NSI - 1:
                roots[p] = matmul_split(y, c)
    for p in range(patches):
        inv_half = inverse[p] / jnp.sqrt(frob[p])
        inner = jnp.sum(inv_half * projected[p], axis=0, keepdims=True)
        mean_weight = jnp.sum(inv_half * inner, axis=1, keepdims=True)
        weights = (jnp.sqrt(float(members - 1)) * inv_half + mean_weight).astype(jnp.bfloat16)
        state = col_ref[:, p].astype(jnp.float32).reshape(members, cells)
        ens_mean = jnp.sum(state, axis=0, keepdims=True) * (1.0 / members)
        deviation = (state - ens_mean).astype(jnp.bfloat16)
        analysed = lax.dot_general(weights, deviation, (((0,), (0,)), ((), ())),
                                   preferred_element_type=jnp.float32)
        out_ref[:, p] = (analysed + ens_mean).reshape(nm, rows, cells).astype(jnp.bfloat16)


def per_device(nm, ns, yb_pert, innov, obs_rinv, obs_count, block_list, loc_weight, state):
    blocks = obs_count.shape[0]
    rows, width = yb_pert.shape
    obs_valid = (jnp.arange(BLOCK, dtype=jnp.int32)[None, :] < obs_count[:, None]).astype(
        jnp.float32
    )
    weighted = (obs_rinv.reshape(blocks, BLOCK) * obs_valid).reshape(-1)
    paired = jnp.stack([innov, weighted])
    patches = block_list.shape[0]
    slots = block_list.shape[2]
    cells = state.shape[3]
    dma = pltpu.SemaphoreType.DMA
    nz = nm // 2
    columns = jnp.transpose(state[:, 0].reshape(rows, nm, patches, cells), (1, 2, 0, 3))
    columns = lax.all_to_all(columns, "mem", split_axis=0, concat_axis=0)
    window, auxw = pl.pallas_call(
        functools.partial(gather_window, nm, ns),
        out_shape=(jax.ShapeDtypeStruct((nm, rows, 3 * width), jnp.bfloat16),
                   jax.ShapeDtypeStruct((3, 2, width), jnp.float32)),
        in_specs=[pl.BlockSpec(memory_space=pl.ANY)] * 2,
        out_specs=[pl.BlockSpec(memory_space=pl.ANY)] * 2,
        scratch_shapes=[dma, dma, dma((nz,)), dma((nz,)), dma((2, nz)), dma((2, nz)),
                        dma((3, nz)), dma((3, nz)), dma((2,)), dma((2,))],
        compiler_params=pltpu.CompilerParams(collective_id=0, has_side_effects=True),
        cost_estimate=pl.CostEstimate(flops=0, bytes_accessed=40 << 20, transcendentals=0),
        name="gather_window",
    )(yb_pert, paired)
    members = nm * rows
    vmem = pl.BlockSpec(memory_space=pltpu.VMEM)
    smem = pl.BlockSpec(memory_space=pltpu.SMEM)
    analysed = pl.pallas_call(
        functools.partial(analyse, blocks),
        out_shape=jax.ShapeDtypeStruct(columns.shape, jnp.bfloat16),
        in_specs=[smem, smem, vmem, vmem, vmem],
        out_specs=vmem,
        scratch_shapes=[pltpu.VMEM((patches, members, slots * BLOCK), jnp.bfloat16)],
        compiler_params=pltpu.CompilerParams(vmem_limit_bytes=48 << 20),
        cost_estimate=pl.CostEstimate(flops=12 << 30, bytes_accessed=16 << 20, transcendentals=0),
        name="analyse",
    )(block_list[:, 0], loc_weight[:, 0], window, auxw, columns)
    back = lax.all_to_all(analysed, "mem", split_axis=0, concat_axis=0)
    return jnp.transpose(back, (2, 0, 1, 3)).reshape(state.shape)


def solution(mesh):
    in_specs = (
        P("mem", "space"),
        P("space"),
        P("space"),
        P("space"),
        P("mem", "space", None),
        P("mem", "space", None),
        P("mem", "space", None, None),
    )
    out_specs = P("mem", "space", None, None)
    return jax.shard_map(
        functools.partial(per_device, mesh.shape["mem"], mesh.shape["space"]),
        mesh=mesh, in_specs=in_specs, out_specs=out_specs, check_vma=False
    )
```

time: 220 us -> 150 us (0.68)
  the two profiles are of different devices: /device:TPU:0 before, /device:TPU:13 now
where the time goes in v1:
time: 150 us; the launch traced here: 147 us
  Pallas kernels  86 us (57%)
  blocking collectives  49.1 us (33%)
  starting transfers between devices  5.78 us (4%)
  local copies, waits for them, and re-layouts  5.16 us (3%)
    pallas_call x1, Pallas kernels, per_device(): pl.pallas_call(functools.partial(gather_window, nm, ns), out_shape=(jax.S...  68.7 us
    all_to_all x1, blocking collectives, per_device(): back = lax.all_to_all(analysed, 'mem', split_axis=0, concat_axis=0)  49.1 us
    pallas_call x1, Pallas kernels, per_device(): pl.pallas_call(functools.partial(analyse, blocks), out_shape=jax.ShapeDty...  17.4 us
    all_to_all x1, starting transfers between devices, per_device(): columns = lax.all_to_all(columns, 'mem', split_axis=0, concat_axis=0)  5.78 us
    unnamed x13, local copies, waits for them, and re-layouts  3.69 us
  transfers between devices with their start and end apart: 1, of which 0 were waited for; matrix products, arithmetic and copies ran while one was open for 0% of the time, Pallas kernels for 47%

profile of v1, /device:TPU:13, one launch (start us, length us, event | category | flops | bytes accessed | tf_op | source)
XLA Modules:
  0.0 146.8 jit_solution(5304486171926494372)
XLA Ops:
  0.0 2.8 %copy.8 = bf16[32,1,32,576]{3,0,2,1:T(8,128)(2,1)} copy(bf16[32,1,32,576]{3,2,1,0:T(8,128)(2,1)} %param.13) | data formatting | bytes 2359296 | tf_op args[6]
  2.8 0.0 copy-start.3
  2.8 0.0 copy-start.5
  2.8 0.0 copy-start.4
  2.8 0.0 copy-start.1
  2.8 0.0 copy-start.2
  2.8 5.8 %all-to-all-start = ((bf16[8,4,32,576]{3,2,1,0:T(8,128)(2,1)}), bf16[8,4,32,576]{3,2,1,0:T(8,128)(2,1)S(1)}, u32[]{:S(2)}, u32[]{:S(2)}) async-start(bf16[8,4,32,576]{3,2,1,0:T(8,128)(2,1)} %bitcast.6), calls=%async_computation | async-start | bytes 2621440 | tf_op jit(solution)/shard_map/all_to_all | solution.py:228
  8.6 0.0 copy-done.3
  8.6 0.0 copy-done.5
  8.6 0.1 fusion.1
  8.7 0.0 copy-done.4
  8.7 0.6 pad_maximum_fusion.aux_ref
  9.3 68.7 %gather_window.1 = (bf16[8,32,12288]{2,1,0:T(8,128)(2,1)}, f32[3,2,4096]{2,1,0:T(2,128)}) custom-call(bf16[32,4096]{1,0:T(8,128)(2,1)} %yb_ref.1, f32[2,4096]{1,0:T(2,128)} %pad_maximum_fusion.aux_ref), custom_call_target="tpu_custom_call" | custom-call | bytes 41943040 | tf_op jit(solution)/shard_map/gather_window/pallas_call | solution.py:229
  78.0 0.0 all-to-all-done.col_ref
  78.0 0.0 copy-done.1
  78.0 0.0 copy-done.2
  78.0 0.0 copy-start
  78.0 0.9 copy-done
  78.9 17.4 %analyse.1 = bf16[8,4,32,576]{3,2,1,0:T(8,128)(2,1)S(1)} custom-call(s32[4,16]{1,0:T(4,128)S(1)} %bitcast.14, f32[4,16]{1,0:T(4,128)S(1)} %bitcast.15, bf16[8,32,12288]{2,1,0:T(8,128)(2,1)} %get-tuple-element.7.win_ref, f32[3,2,4096]{2,1,0:T(2,128)S(1)} %copy-done, bf16[8,4,32,576]{3,2,1,0:T(8,128)(2,1)S(1)} %all-to-all-done.col_ref), custom_call_target="tpu_custom_call" | custom-call | flops 12884901888 | bytes 16777216 | tf_op jit(solution)/shard_map/analyse/pallas_call | solution.py:244
  96.3 49.1 %all_to_all.10 = bf16[8,4,32,576]{3,2,1,0:T(8,128)(2,1)S(1)} all-to-all(bf16[8,4,32,576]{3,2,1,0:T(8,128)(2,1)S(1)} %analyse.1), channel_id=1, replica_groups=mesh['mem'=8,'space'=4] {'mem'}, dimensions={0} | all-to-all | bytes 2359296 | tf_op jit(solution)/shard_map/all_to_all | solution.py:254
  145.4 1.5 %copy.9 = bf16[32,1,32,576]{3,2,1,0:T(8,128)(2,1)} copy(bf16[32,1,32,576]{3,0,2,1:T(8,128)(2,1)S(1)} %bitcast.16) | data formatting | bytes 2359296 | tf_op jit(solution)/shard_map/reshape | solution.py:255
Async XLA Ops:
  2.8 5.8 %copy-start.3 = (f32[4096]{0:T(1024)S(1)}, f32[4096]{0:T(1024)}, u32[]{:S(2)}) copy-start(f32[4096]{0:T(1024)} %param.9) | copy-start | bytes 49156
  2.8 5.8 %copy-start.5 = (s32[32]{0:T(128)S(1)}, s32[32]{0:T(128)}, u32[]{:S(2)}) copy-start(s32[32]{0:T(128)} %param.10) | copy-start | bytes 388
  2.8 5.9 %copy-start.4 = (f32[4096]{0:T(1024)S(1)}, f32[4096]{0:T(1024)}, u32[]{:S(2)}) copy-start(f32[4096]{0:T(1024)} %param.8) | copy-start | bytes 49156
  2.8 75.2 %copy-start.1 = (s32[4,1,16]{2,1,0:T(1,128)S(1)}, s32[4,1,16]{2,1,0:T(1,128)}, u32[]{:S(2)}) copy-start(s32[4,1,16]{2,1,0:T(1,128)} %param.11) | copy-start | bytes 772
  2.8 75.2 %copy-start.2 = (f32[4,1,16]{2,1,0:T(1,128)S(1)}, f32[4,1,16]{2,1,0:T(1,128)}, u32[]{:S(2)}) copy-start(f32[4,1,16]{2,1,0:T(1,128)} %param.12) | copy-start | bytes 772
  2.8 75.2 %all-to-all-start = ((bf16[8,4,32,576]{3,2,1,0:T(8,128)(2,1)}), bf16[8,4,32,576]{3,2,1,0:T(8,128)(2,1)S(1)}, u32[]{:S(2)}, u32[]{:S(2)}) async-start(bf16[8,4,32,576]{3,2,1,0:T(8,128)(2,1)} %bitcast.6), calls=%async_computation | async-start | bytes 2621440 | tf_op jit(solution)/shard_map/all_to_all | solution.py:228
  78.0 0.9 copy-start

commit v2 on v1

v2 whole, which is shorter than its diff:
```python
import functools

import jax
import jax.numpy as jnp
from jax import lax
from jax.experimental import pallas as pl
from jax.experimental.pallas import tpu as pltpu
from jax.sharding import PartitionSpec as P

BLOCK = 128
NSI = 6
RELAYED = (1, 2)
MESH = pl.DeviceIdType.MESH


inflation = 1.1


def gather_window(nm, ns, yb_ref, aux_ref, cut_ref, win_ref, auxw_ref, col_ref, relay_ref,
                  local_sem, local_aux_sem, local_state_sem, sz, rz, sx, rx, sc, rc, sa, ra,
                  ss, rs, sr, rr):
    mem = lax.axis_index("mem")
    strip = lax.axis_index("space")
    nz = nm // 2
    z, core = mem // 2, lax.rem(mem, 2)
    other = mem + 1 - 2 * core
    width = yb_ref.shape[1]

    def place(index, slot):
        return win_ref.at[index, :, pl.ds(slot * width, width)]

    def peer(step):
        return lax.rem(z + step, nz) * 2 + core

    has = (strip > 0, strip < ns - 1)
    beside = (strip - 1, strip + 1)
    relayed = RELAYED if ns == 4 else ()
    inner = jnp.logical_or(strip == 1, strip == 2)
    facing = lax.rem(strip + 2, ns)

    barrier = pltpu.get_barrier_semaphore()
    for step in range(1, nm):
        pl.semaphore_signal(barrier, inc=1, device_id=(lax.rem(mem + step, nm), strip),
                            device_id_type=MESH)
    for side in range(2):
        @pl.when(has[side])
        def _():
            pl.semaphore_signal(barrier, inc=1, device_id=(mem, beside[side]), device_id_type=MESH)
    if relayed:
        pl.semaphore_signal(barrier, inc=1, device_id=(mem, facing), device_id_type=MESH)
    pl.semaphore_wait(
        barrier,
        nm - 1 + bool(relayed) + has[0].astype(jnp.int32) + has[1].astype(jnp.int32))

    keep = pltpu.make_async_copy(yb_ref, place(mem, 1), local_sem)
    keep_aux = pltpu.make_async_copy(aux_ref, auxw_ref.at[1], local_aux_sem)

    keep_state = pltpu.make_async_copy(cut_ref.at[mem], col_ref.at[mem], local_state_sem)

    def state_out(step):
        to = lax.rem(mem + step, nm)
        return pltpu.make_async_remote_copy(
            cut_ref.at[to], col_ref.at[mem], ss.at[step], rs.at[step],
            device_id=(to, strip), device_id_type=MESH)

    def state_in(step):
        source = lax.rem(mem + nm - step, nm)
        return pltpu.make_async_remote_copy(
            cut_ref.at[source], col_ref.at[source], ss.at[step], rs.at[step],
            device_id=(source, strip), device_id_type=MESH)

    def along(step):
        return pltpu.make_async_remote_copy(
            yb_ref, place(mem, 1), sz.at[step], rz.at[step],
            device_id=(peer(step), strip), device_id_type=MESH)

    def across(step, side):
        index = peer(step)
        return pltpu.make_async_remote_copy(
            yb_ref if step == 0 else place(index, 1), place(index, 2 - 2 * side),
            sx.at[side, step], rx.at[side, step],
            device_id=(mem, beside[side]), device_id_type=MESH)

    def arrive(step, side):
        index = peer(step)
        spot = place(index, 2 * side)
        return pltpu.make_async_remote_copy(
            spot, spot, sx.at[1 - side, step], rx.at[1 - side, step],
            device_id=(mem, beside[side]), device_id_type=MESH)

    def arrive_along(step):
        spot = place(peer(nz - step), 1)
        return pltpu.make_async_remote_copy(
            spot, spot, sz.at[step], rz.at[step],
            device_id=(peer(nz - step), strip), device_id_type=MESH)

    def over(step, slot):
        index = peer(step)
        return pltpu.make_async_remote_copy(
            yb_ref if step == 0 and slot == 1 else place(index, slot), place(index, slot),
            sc.at[slot, step], rc.at[slot, step],
            device_id=(other, strip), device_id_type=MESH)

    def arrive_over(step, slot):
        spot = place(lax.rem(z + step, nz) * 2 + 1 - core, slot)
        return pltpu.make_async_remote_copy(
            spot, spot, sc.at[slot, step], rc.at[slot, step],
            device_id=(other, strip), device_id_type=MESH)

    def beside_aux(side):
        return pltpu.make_async_remote_copy(
            aux_ref, auxw_ref.at[2 - 2 * side], sa.at[side], ra.at[side],
            device_id=(mem, beside[side]), device_id_type=MESH)

    def arrive_aux(side):
        return pltpu.make_async_remote_copy(
            aux_ref, auxw_ref.at[2 * side], sa.at[1 - side], ra.at[1 - side],
            device_id=(mem, beside[side]), device_id_type=MESH)

    def first_leg(step):
        index = peer(step)
        return pltpu.make_async_remote_copy(
            yb_ref if step == 0 else place(index, 1), relay_ref.at[relayed.index(step)],
            sr.at[relayed.index(step)], rr.at[relayed.index(step)],
            device_id=(mem, facing), device_id_type=MESH)

    def second_leg(step, side):
        return pltpu.make_async_remote_copy(
            relay_ref.at[relayed.index(step)], place(peer(step), 2 - 2 * side),
            sr.at[relayed.index(step)], rx.at[side, step],
            device_id=(mem, (1, 2)[side]), device_id_type=MESH)

    def direct(step, side):
        if step not in relayed:
            return has[side]
        return jnp.logical_and(has[side], strip != (2, 1)[side])

    def send_across(step):
        for side in range(2):
            @pl.when(direct(step, side))
            def _():
                across(step, side).start()
        if step in relayed:
            @pl.when(inner)
            def _():
                first_leg(step).start()

    def pass_on(step):
        if step in relayed:
            for side in range(2):
                @pl.when(strip == (0, 3)[side])
                def _():
                    first_leg(step).wait_recv()
                    second_leg(step, side).start()

    for step in range(1, nz):
        along(step).start()
    send_across(0)
    keep.start()
    keep_aux.start()
    over(0, 1).start()
    for side in range(2):
        @pl.when(has[side])
        def _():
            beside_aux(side).start()
    order = [nz - step for step in range(1, nz)]
    for step in range(1, nz):
        arrive_along(step).wait_recv()
        send_across(nz - step)
        over(nz - step, 1).start()
    for step in sorted(range(1, nm), key=lambda step: -min(step, nm - step)):
        state_out(step).start()
    keep_state.start()
    for step in [0] + order:
        pass_on(step)
        for side in range(2):
            @pl.when(has[side])
            def _():
                arrive(step, side).wait_recv()
                over(step, 2 * side).start()
    keep.wait()
    keep_aux.wait()
    keep_state.wait()
    for step in range(1, nm):
        state_out(step).wait_send()
        state_in(step).wait_recv()
    for step in range(1, nz):
        along(step).wait_send()
    for step in [0] + order:
        over(step, 1).wait_send()
        arrive_over(step, 1).wait_recv()
        if step in relayed:
            @pl.when(inner)
            def _():
                first_leg(step).wait_send()
            for side in range(2):
                @pl.when(strip == (0, 3)[side])
                def _():
                    second_leg(step, side).wait_send()
        for side in range(2):
            @pl.when(direct(step, side))
            def _():
                across(step, side).wait_send()

            @pl.when(has[side])
            def _():
                over(step, 2 * side).wait_send()
                arrive_over(step, 2 * side).wait_recv()
    for side in range(2):
        @pl.when(has[side])
        def _():
            beside_aux(side).wait_send()
            arrive_aux(side).wait_recv()


def split(value):
    high = value.astype(jnp.bfloat16)
    return high, (value - high.astype(jnp.float32)).astype(jnp.bfloat16)


def matmul_split(left, right):
    (lh, ll), (rh, rl) = left, right
    return jnp.dot(jnp.concatenate([lh, lh, ll], axis=1),
                   jnp.concatenate([rh, rl, rh], axis=0),
                   preferred_element_type=jnp.float32)


def gram_of_patches(blocks, list_ref, loc_ref, win_ref, aux_ref, system_ref, proj_ref,
                    scaled_ref):
    patches, slots = list_ref.shape
    members = system_ref.shape[1]
    identity = (lax.broadcasted_iota(jnp.int32, (members, members), 0)
                == lax.broadcasted_iota(jnp.int32, (members, members), 1)).astype(jnp.float32)
    for p in range(patches):
        def slot_body(j, acc):
            q = list_ref[p, j]
            live = (q >= 0).astype(jnp.float32)
            q = jnp.where(q >= 0, q, blocks)
            lanes = pl.ds(pl.multiple_of(q * BLOCK, BLOCK), BLOCK)
            inner = pl.ds(pl.multiple_of(lax.rem(q, blocks) * BLOCK, BLOCK), BLOCK)
            aux = aux_ref[q // blocks, :, inner]
            root = jnp.sqrt(aux[1:2, :] * (loc_ref[p, j] * live))
            chunk = win_ref[:, :, lanes].astype(jnp.float32).reshape(members, BLOCK)
            scaled = (chunk * root).astype(jnp.bfloat16)
            scaled_ref[p, :, pl.ds(pl.multiple_of(j * BLOCK, BLOCK), BLOCK)] = scaled
            return acc + scaled.astype(jnp.float32) * (root * aux[0:1, :])
        acc = lax.fori_loop(0, slots, slot_body, jnp.zeros((members, BLOCK), jnp.float32),
                            unroll=4)
        proj_ref[p] = jnp.sum(acc, axis=1, keepdims=True)
        scaled = scaled_ref[p]
        gram = lax.dot_general(scaled, scaled, (((1,), (1,)), ((), ())),
                               preferred_element_type=jnp.float32)
        system_ref[p] = gram + (members - 1) / inflation * identity


def analyse(cells, system_ref, proj_ref, col_ref, back_ref, out_ref, local_sem, send_sem,
            recv_sem):
    nm, rows, total = col_ref.shape
    patches = system_ref.shape[0]
    members = nm * rows
    group = 2
    span = group * cells
    mem, strip = lax.axis_index("mem"), lax.axis_index("space")
    barrier = pltpu.get_barrier_semaphore()
    for step in range(1, nm):
        pl.semaphore_signal(barrier, inc=1, device_id=(lax.rem(mem + step, nm), strip),
                            device_id_type=MESH)
    pl.semaphore_wait(barrier, nm - 1)
    identity = (lax.broadcasted_iota(jnp.int32, (members, members), 0)
                == lax.broadcasted_iota(jnp.int32, (members, members), 1)).astype(jnp.float32)

    def returned(first, step):
        to = lax.rem(mem + step, nm)
        lanes = pl.ds(first * cells, span)
        return pltpu.make_async_remote_copy(
            out_ref.at[to, :, lanes], back_ref.at[mem, :, lanes],
            send_sem.at[first // group, step], recv_sem.at[first // group, step],
            device_id=(to, strip), device_id_type=MESH)

    def received(first, step):
        source = lax.rem(mem + nm - step, nm)
        spot = back_ref.at[source, :, pl.ds(first * cells, span)]
        return pltpu.make_async_remote_copy(
            spot, spot, send_sem.at[first // group, step], recv_sem.at[first // group, step],
            device_id=(source, strip), device_id_type=MESH)

    steps = sorted(range(1, nm), key=lambda step: -min(step, nm - step))
    for first in range(0, patches, group):
        here = range(group)
        systems = [system_ref[first + p] for p in here]
        projected = [proj_ref[first + p] for p in here]
        frob = [jnp.sqrt(jnp.sum(s * s, keepdims=True)) for s in systems]
        roots = [s / f for s, f in zip(systems, frob)]
        inverse = [None] * group
        for iteration in range(NSI):
            for p in here:
                y = split(roots[p])
                if iteration == 0:
                    correction = 1.5 * identity - 0.5 * roots[p]
                    c = split(correction)
                    inverse[p] = correction
                else:
                    v = split(inverse[p])
                    correction = 1.5 * identity - 0.5 * matmul_split(v, y)
                    c = split(correction)
                    inverse[p] = matmul_split(c, v)
                if iteration < NSI - 1:
                    roots[p] = matmul_split(y, c)
        lanes = slice(first * cells, first * cells + span)
        state = col_ref[:, :, lanes].astype(jnp.float32).reshape(members, span)
        ens_mean = jnp.sum(state, axis=0, keepdims=True) * (1.0 / members)
        deviation = (state - ens_mean).astype(jnp.bfloat16)
        analysed = []
        for p in here:
            inv_half = inverse[p] / jnp.sqrt(frob[p])
            inner = jnp.sum(inv_half * projected[p], axis=0, keepdims=True)
            mean_weight = jnp.sum(inv_half * inner, axis=1, keepdims=True)
            weights = (jnp.sqrt(float(members - 1)) * inv_half + mean_weight).astype(jnp.bfloat16)
            analysed.append(lax.dot_general(
                weights, deviation[:, p * cells:(p + 1) * cells], (((0,), (0,)), ((), ())),
                preferred_element_type=jnp.float32))
        result = jnp.concatenate(analysed, axis=1) + ens_mean
        out_ref[:, :, lanes] = result.reshape(nm, rows, span).astype(jnp.bfloat16)
        for step in steps:
            returned(first, step).start()
    keep = pltpu.make_async_copy(out_ref.at[mem], back_ref.at[mem], local_sem)
    keep.start()
    keep.wait()
    for first in range(0, patches, group):
        for step in steps:
            returned(first, step).wait_send()
            received(first, step).wait_recv()


def per_device(nm, ns, yb_pert, innov, obs_rinv, obs_count, block_list, loc_weight, state):
    blocks = obs_count.shape[0]
    rows, width = yb_pert.shape
    obs_valid = (jnp.arange(BLOCK, dtype=jnp.int32)[None, :] < obs_count[:, None]).astype(
        jnp.float32
    )
    weighted = (obs_rinv.reshape(blocks, BLOCK) * obs_valid).reshape(-1)
    paired = jnp.stack([innov, weighted])
    patches = block_list.shape[0]
    slots = block_list.shape[2]
    cells = state.shape[3]
    dma = pltpu.SemaphoreType.DMA
    nz = nm // 2
    columns = jnp.transpose(state[:, 0].reshape(rows, nm, patches * cells), (1, 0, 2))
    window, auxw, columns, _ = pl.pallas_call(
        functools.partial(gather_window, nm, ns),
        out_shape=(jax.ShapeDtypeStruct((nm, rows, 3 * width), jnp.bfloat16),
                   jax.ShapeDtypeStruct((3, 2, width), jnp.float32),
                   jax.ShapeDtypeStruct(columns.shape, jnp.bfloat16),
                   jax.ShapeDtypeStruct((len(RELAYED), rows, width), jnp.bfloat16)),
        in_specs=[pl.BlockSpec(memory_space=pl.ANY)] * 3,
        out_specs=[pl.BlockSpec(memory_space=pl.ANY)] * 4,
        scratch_shapes=[dma, dma, dma, dma((nz,)), dma((nz,)), dma((2, nz)), dma((2, nz)),
                        dma((3, nz)), dma((3, nz)), dma((2,)), dma((2,)), dma((nm,)), dma((nm,)), dma((len(RELAYED),)),
                        dma((len(RELAYED),))],
        compiler_params=pltpu.CompilerParams(collective_id=0, has_side_effects=True),
        cost_estimate=pl.CostEstimate(flops=0, bytes_accessed=40 << 20, transcendentals=0),
        name="gather_window",
    )(yb_pert, paired, columns)
    members = nm * rows
    vmem = pl.BlockSpec(memory_space=pltpu.VMEM)
    smem = pl.BlockSpec(memory_space=pltpu.SMEM)
    systems, projected = pl.pallas_call(
        functools.partial(gram_of_patches, blocks),
        out_shape=(jax.ShapeDtypeStruct((patches, members, members), jnp.float32),
                   jax.ShapeDtypeStruct((patches, members, 1), jnp.float32)),
        in_specs=[smem, smem, vmem, vmem],
        out_specs=[vmem, vmem],
        scratch_shapes=[pltpu.VMEM((patches, members, slots * BLOCK), jnp.bfloat16)],
        compiler_params=pltpu.CompilerParams(vmem_limit_bytes=48 << 20),
        cost_estimate=pl.CostEstimate(flops=2 << 30, bytes_accessed=8 << 20, transcendentals=0),
        name="gram_of_patches",
    )(block_list[:, 0], loc_weight[:, 0], window, auxw)
    back = pl.pallas_call(
        functools.partial(analyse, cells),
        out_shape=jax.ShapeDtypeStruct(columns.shape, jnp.bfloat16),
        in_specs=[vmem, vmem, vmem],
        out_specs=pl.BlockSpec(memory_space=pl.ANY),
        scratch_shapes=[pltpu.VMEM(columns.shape, jnp.bfloat16),
                        dma, dma((patches // 2, nm)), dma((patches // 2, nm))],
        compiler_params=pltpu.CompilerParams(
            collective_id=1, has_side_effects=True, vmem_limit_bytes=48 << 20),
        cost_estimate=pl.CostEstimate(flops=8 << 30, bytes_accessed=8 << 20, transcendentals=0),
        name="analyse",
    )(systems, projected, columns)
    return jnp.transpose(back, (1, 0, 2)).reshape(state.shape)


def solution(mesh):
    in_specs = (
        P("mem", "space"),
        P("space"),
        P("space"),
        P("space"),
        P("mem", "space", None),
        P("mem", "space", None),
        P("mem", "space", None, None),
    )
    out_specs = P("mem", "space", None, None)
    return jax.shard_map(
        functools.partial(per_device, mesh.shape["mem"], mesh.shape["space"]),
        mesh=mesh, in_specs=in_specs, out_specs=out_specs, check_vma=False
    )
```

time: 150 us -> 116 us (0.77); the launches traced: 147 us -> 115 us
  blocking collectives: 49.1 us -> 0 us
  Pallas kernels: 86 us -> 105 us
  starting transfers between devices: 5.78 us -> 0 us
  local copies, waits for them, and re-layouts: 5.16 us -> 7.88 us
    all_to_all x1 -> x0, blocking collectives: 49.1 us -> none  [per_device(): back = lax.all_to_all(analysed, 'mem', split_axis=0, concat_axis=0)]
    pallas_call x1 -> x2, Pallas kernels: 17.4 us -> 53.2 us  [the longest x1 45.6 us: per_device(): pl.pallas_call(functools.partial(analyse, cells), out_shape=jax.ShapeDtyp...]
    pallas_call x1, Pallas kernels: 68.7 us -> 51.8 us  [per_device(): pl.pallas_call(functools.partial(gather_window, nm, ns), out_shape=(jax.S...]
    all_to_all x1 -> x0, starting transfers between devices: 5.78 us -> none  [per_device(): columns = lax.all_to_all(columns, 'mem', split_axis=0, concat_axis=0)]
    another operation x0 -> x2, local copies, waits for them, and re-layouts: none -> 3.93 us  [per_device(): state[:, 0].reshape(rows, nm, patches * cells)]
    unnamed x13 -> x8, local copies, waits for them, and re-layouts: 3.69 us -> 0.9 us
  transfers between devices with their start and end apart: 1 -> 0, of which waited for: 0 -> 0; matrix products, arithmetic and copies ran while one was open for 0% -> 0% of each run, Pallas kernels for 47% -> 0%
where the time goes in v2:
time: 116 us; the launch traced here: 115 us
  Pallas kernels  105 us (91%)
  local copies, waits for them, and re-layouts  7.88 us (7%)
  other arithmetic  2.14 us (2%)
    pallas_call x1, Pallas kernels, per_device(): pl.pallas_call(functools.partial(gather_window, nm, ns), out_shape=(jax.S...  51.8 us
    pallas_call x1, Pallas kernels, per_device(): pl.pallas_call(functools.partial(analyse, cells), out_shape=jax.ShapeDtyp...  45.6 us
    pallas_call x1, Pallas kernels, per_device(): pl.pallas_call(functools.partial(gram_of_patches, blocks), out_shape=(jax...  7.65 us
    another operation x2, local copies, waits for them, and re-layouts, per_device(): state[:, 0].reshape(rows, nm, patches * cells)  3.93 us
    reshape x1, local copies, waits for them, and re-layouts, per_device(): return jnp.transpose(back, (1, 0, 2)).reshape(state.shape)  2.4 us

profile of v2, /device:TPU:13, one launch (start us, length us, event | category | flops | bytes accessed | tf_op | source)
XLA Modules:
  0.0 115.2 jit_solution(11286574924489012516)
XLA Ops:
  0.0 0.8 fusion.1
  0.8 1.4 %pad_maximum_fusion.aux_ref = f32[2,4096]{1,0:T(2,128)} fusion(f32[1,4096]{1,0:T(1,128)S(1)} %bitcast.19, f32[1,4096]{1,0:T(1,128)} %bitcast.20), kind=kLoop, calls=%fused_computation.1 | loop fusion | flops 8192 | bytes 65536 | tf_op jit(solution)/shard_map/stack | solution.py:342
  2.1 2.7 %reshape_squeeze.3 = bf16[32,8,2304]{2,1,0:T(8,128)(2,1)S(1)} reshape(bf16[32,1,32,576]{3,2,1,0:T(8,128)(2,1)} %param.13) | data formatting | bytes 2359296 | tf_op jit(solution)/shard_map/reshape;squeeze | solution.py:348
  4.9 1.2 %copy.12 = bf16[32,8,2304]{2,0,1:T(8,128)(2,1)} copy(bf16[32,8,2304]{2,1,0:T(8,128)(2,1)S(1)} %reshape_squeeze.3) | data formatting | bytes 2359296 | tf_op jit(solution)/shard_map/reshape;squeeze | solution.py:348
  6.1 0.0 copy-start.2
  6.1 0.0 copy-start.3
  6.1 51.8 %gather_window.1 = (bf16[8,32,12288]{2,1,0:T(8,128)(2,1)}, f32[3,2,4096]{2,1,0:T(2,128)}, bf16[8,32,2304]{2,1,0:T(8,128)(2,1)}, bf16[2,32,4096]{2,1,0:T(8,128)(2,1)}) custom-call(bf16[32,4096]{1,0:T(8,128)(2,1)} %yb_ref.1, f32[2,4096]{1,0:T(2,128)} %pad_maximum_fusion.aux_ref, bf16[8,32,2304]{2,1,0:T(8,128)(2,1)} %bitcast.18), custom_call_target="tpu_custom_call" | custom-call | bytes 41943040 | tf_op jit(solution)/shard_map/gather_window/pallas_call | solution.py:349
  57.9 0.0 copy-done.2
  57.9 0.0 copy-done.3
  58.0 0.0 copy-start.1
  58.0 0.9 copy-done.1
  58.8 0.0 copy-start
  58.9 7.6 %gram_of_patches.1 = (f32[4,256,256]{2,1,0:T(8,128)S(1)}, f32[4,256,1]{2,1,0:T(8,128)S(1)}) custom-call(s32[4,16]{1,0:T(4,128)S(1)} %bitcast.16, f32[4,16]{1,0:T(4,128)S(1)} %bitcast.17, bf16[8,32,12288]{2,1,0:T(8,128)(2,1)} %get-tuple-element.10.win_ref, f32[3,2,4096]{2,1,0:T(2,128)S(1)} %copy-done.1), custom_call_target="tpu_custom_call" | custom-call | flops 2147483648 | bytes 8388608 | tf_op jit(solution)/shard_map/gram_of_patches/pallas_call | solution.py:367
  66.5 0.0 copy-done
  66.5 45.6 %analyse.1 = bf16[8,32,2304]{2,1,0:T(8,128)(2,1)S(1)} custom-call(f32[4,256,256]{2,1,0:T(8,128)S(1)} %get-tuple-element.12.system_ref, f32[4,256,1]{2,1,0:T(8,128)S(1)} %get-tuple-element.13.proj_ref, bf16[8,32,2304]{2,1,0:T(8,128)(2,1)S(1)} %copy-done), custom_call_target="tpu_custom_call" | custom-call | flops 8589934592 | bytes 8388608 | tf_op jit(solution)/shard_map/analyse/pallas_call | solution.py:378
  112.1 0.7 copy.9
  112.8 2.4 %reshape.17 = bf16[32,1,32,576]{3,2,0,1:T(8,128)(2,1)} reshape(bf16[32,8,2304]{2,1,0:T(8,128)(2,1)S(1)} %copy.9) | data formatting | bytes 2359296 | tf_op jit(solution)/shard_map/reshape | solution.py:390
Async XLA Ops:
  6.1 51.9 %copy-start.2 = (s32[4,1,16]{2,1,0:T(1,128)S(1)}, s32[4,1,16]{2,1,0:T(1,128)}, u32[]{:S(2)}) copy-start(s32[4,1,16]{2,1,0:T(1,128)} %param.11) | copy-start | bytes 772
  6.1 51.9 %copy-start.3 = (f32[4,1,16]{2,1,0:T(1,128)S(1)}, f32[4,1,16]{2,1,0:T(1,128)}, u32[]{:S(2)}) copy-start(f32[4,1,16]{2,1,0:T(1,128)} %param.12) | copy-start | bytes 772
  58.0 0.9 copy-start.1
  58.8 7.7 %copy-start = (bf16[8,32,2304]{2,1,0:T(8,128)(2,1)S(1)}, bf16[8,32,2304]{2,1,0:T(8,128)(2,1)}, u32[]{:S(2)}) copy-start(bf16[8,32,2304]{2,1,0:T(8,128)(2,1)} %get-tuple-element.14.col_ref) | copy-start | bytes 3538948

commit v3 on v2

--- a/solution.py
+++ b/solution.py
@@ -55,24 +55,38 @@
     keep = pltpu.make_async_copy(yb_ref, place(mem, 1), local_sem)
     keep_aux = pltpu.make_async_copy(aux_ref, auxw_ref.at[1], local_aux_sem)
 
-    keep_state = pltpu.make_async_copy(cut_ref.at[mem], col_ref.at[mem], local_state_sem)
+    span = col_ref.shape[2]
+
+    def cut(index):
+        return cut_ref.at[:, pl.ds(pl.multiple_of(index * span, BLOCK), span)]
+
+    keep_state = pltpu.make_async_copy(cut(mem), col_ref.at[mem], local_state_sem)
 
     def state_out(step):
         to = lax.rem(mem + step, nm)
         return pltpu.make_async_remote_copy(
-            cut_ref.at[to], col_ref.at[mem], ss.at[step], rs.at[step],
+            cut(to), col_ref.at[mem], ss.at[step], rs.at[step],
             device_id=(to, strip), device_id_type=MESH)
 
     def state_in(step):
         source = lax.rem(mem + nm - step, nm)
         return pltpu.make_async_remote_copy(
-            cut_ref.at[source], col_ref.at[source], ss.at[step], rs.at[step],
+            cut(source), col_ref.at[source], ss.at[step], rs.at[step],
             device_id=(source, strip), device_id_type=MESH)
 
-    def along(step):
-        return pltpu.make_async_remote_copy(
-            yb_ref, place(mem, 1), sz.at[step], rz.at[step],
-            device_id=(peer(step), strip), device_id_type=MESH)
+    def along(way, hop):
+        sign = (1, -1)[way]
+        spot = place((z - sign * hop) * 2 + core, 1)
+        return pltpu.make_async_remote_copy(
+            yb_ref if hop == 0 else spot, spot, sz.at[way, hop], rz.at[way, hop],
+            device_id=((z + sign) * 2 + core, strip), device_id_type=MESH)
+
+    def goes(way, hop):
+        return (jnp.logical_and(z >= hop, z < nz - 1) if way == 0
+                else jnp.logical_and(z + hop < nz, z > 0))
+
+    def comes(way, hop):
+        return z >= hop + 1 if way == 0 else z + hop + 1 < nz
 
     def across(step, side):
         index = peer(step)
@@ -88,11 +102,12 @@
             spot, spot, sx.at[1 - side, step], rx.at[1 - side, step],
             device_id=(mem, beside[side]), device_id_type=MESH)
 
-    def arrive_along(step):
-        spot = place(peer(nz - step), 1)
-        return pltpu.make_async_remote_copy(
-            spot, spot, sz.at[step], rz.at[step],
-            device_id=(peer(nz - step), strip), device_id_type=MESH)
+    def arrive_along(way, hop):
+        sign = (1, -1)[way]
+        spot = place((z - sign * (hop + 1)) * 2 + core, 1)
+        return pltpu.make_async_remote_copy(
+            spot, spot, sz.at[way, hop], rz.at[way, hop],
+            device_id=((z - sign) * 2 + core, strip), device_id_type=MESH)
 
     def over(step, slot):
         index = peer(step)
@@ -153,8 +168,10 @@
                     first_leg(step).wait_recv()
                     second_leg(step, side).start()
 
-    for step in range(1, nz):
-        along(step).start()
+    for way in range(2):
+        @pl.when(goes(way, 0))
+        def _():
+            along(way, 0).start()
     send_across(0)
     keep.start()
     keep_aux.start()
@@ -163,11 +180,22 @@
         @pl.when(has[side])
         def _():
             beside_aux(side).start()
-    order = [nz - step for step in range(1, nz)]
-    for step in range(1, nz):
-        arrive_along(step).wait_recv()
-        send_across(nz - step)
-        over(nz - step, 1).start()
+    order = sorted(range(1, nz), key=lambda step: min(step, nz - step))
+    for hop in range(nz - 1):
+        for way in range(2):
+            if hop + 1 < nz - 1:
+                onward = goes(way, hop + 1)
+            step = (nz - 1 - hop, 1 + hop)[way]
+
+            @pl.when(comes(way, hop))
+            def _():
+                arrive_along(way, hop).wait_recv()
+                if hop + 1 < nz - 1:
+                    @pl.when(onward)
+                    def _():
+                        along(way, hop + 1).start()
+                send_across(step)
+                over(step, 1).start()
     for step in sorted(range(1, nm), key=lambda step: -min(step, nm - step)):
         state_out(step).start()
     keep_state.start()
@@ -184,8 +212,11 @@
     for step in range(1, nm):
         state_out(step).wait_send()
         state_in(step).wait_recv()
-    for step in range(1, nz):
-        along(step).wait_send()
+    for hop in range(nz - 1):
+        for way in range(2):
+            @pl.when(goes(way, hop))
+            def _():
+                along(way, hop).wait_send()
     for step in [0] + order:
         over(step, 1).wait_send()
         arrive_over(step, 1).wait_recv()
@@ -269,19 +300,22 @@
     identity = (lax.broadcasted_iota(jnp.int32, (members, members), 0)
                 == lax.broadcasted_iota(jnp.int32, (members, members), 1)).astype(jnp.float32)
 
+    def spot(index, first, length):
+        start = pl.multiple_of(index * total + first * cells, BLOCK)
+        return back_ref.at[:, pl.ds(start, length)]
+
     def returned(first, step):
         to = lax.rem(mem + step, nm)
-        lanes = pl.ds(first * cells, span)
-        return pltpu.make_async_remote_copy(
-            out_ref.at[to, :, lanes], back_ref.at[mem, :, lanes],
+        return pltpu.make_async_remote_copy(
+            out_ref.at[to, :, pl.ds(first * cells, span)], spot(mem, first, span),
             send_sem.at[first // group, step], recv_sem.at[first // group, step],
             device_id=(to, strip), device_id_type=MESH)
 
     def received(first, step):
         source = lax.rem(mem + nm - step, nm)
-        spot = back_ref.at[source, :, pl.ds(first * cells, span)]
-        return pltpu.make_async_remote_copy(
-            spot, spot, send_sem.at[first // group, step], recv_sem.at[first // group, step],
+        landed = spot(source, first, span)
+        return pltpu.make_async_remote_copy(
+            landed, landed, send_sem.at[first // group, step], recv_sem.at[first // group, step],
             device_id=(source, strip), device_id_type=MESH)
 
     steps = sorted(range(1, nm), key=lambda step: -min(step, nm - step))
@@ -323,7 +357,7 @@
         out_ref[:, :, lanes] = result.reshape(nm, rows, span).astype(jnp.bfloat16)
         for step in steps:
             returned(first, step).start()
-    keep = pltpu.make_async_copy(out_ref.at[mem], back_ref.at[mem], local_sem)
+    keep = pltpu.make_async_copy(out_ref.at[mem], spot(mem, 0, total), local_sem)
     keep.start()
     keep.wait()
     for first in range(0, patches, group):
@@ -345,22 +379,22 @@
     cells = state.shape[3]
     dma = pltpu.SemaphoreType.DMA
     nz = nm // 2
-    columns = jnp.transpose(state[:, 0].reshape(rows, nm, patches * cells), (1, 0, 2))
+    flat = state.reshape(rows, nm * patches * cells)
     window, auxw, columns, _ = pl.pallas_call(
         functools.partial(gather_window, nm, ns),
         out_shape=(jax.ShapeDtypeStruct((nm, rows, 3 * width), jnp.bfloat16),
                    jax.ShapeDtypeStruct((3, 2, width), jnp.float32),
-                   jax.ShapeDtypeStruct(columns.shape, jnp.bfloat16),
+                   jax.ShapeDtypeStruct((nm, rows, patches * cells), jnp.bfloat16),
                    jax.ShapeDtypeStruct((len(RELAYED), rows, width), jnp.bfloat16)),
         in_specs=[pl.BlockSpec(memory_space=pl.ANY)] * 3,
         out_specs=[pl.BlockSpec(memory_space=pl.ANY)] * 4,
-        scratch_shapes=[dma, dma, dma, dma((nz,)), dma((nz,)), dma((2, nz)), dma((2, nz)),
+        scratch_shapes=[dma, dma, dma, dma((2, nz)), dma((2, nz)), dma((2, nz)), dma((2, nz)),
                         dma((3, nz)), dma((3, nz)), dma((2,)), dma((2,)), dma((nm,)), dma((nm,)), dma((len(RELAYED),)),
                         dma((len(RELAYED),))],
         compiler_params=pltpu.CompilerParams(collective_id=0, has_side_effects=True),
         cost_estimate=pl.CostEstimate(flops=0, bytes_accessed=40 << 20, transcendentals=0),
         name="gather_window",
-    )(yb_pert, paired, columns)
+    )(yb_pert, paired, flat)
     members = nm * rows
     vmem = pl.BlockSpec(memory_space=pltpu.VMEM)
     smem = pl.BlockSpec(memory_space=pltpu.SMEM)
@@ -377,7 +411,7 @@
     )(block_list[:, 0], loc_weight[:, 0], window, auxw)
     back = pl.pallas_call(
         functools.partial(analyse, cells),
-        out_shape=jax.ShapeDtypeStruct(columns.shape, jnp.bfloat16),
+        out_shape=jax.ShapeDtypeStruct(flat.shape, jnp.bfloat16),
         in_specs=[vmem, vmem, vmem],
         out_specs=pl.BlockSpec(memory_space=pl.ANY),
         scratch_shapes=[pltpu.VMEM(columns.shape, jnp.bfloat16),
@@ -387,7 +421,7 @@
         cost_estimate=pl.CostEstimate(flops=8 << 30, bytes_accessed=8 << 20, transcendentals=0),
         name="analyse",
     )(systems, projected, columns)
-    return jnp.transpose(back, (1, 0, 2)).reshape(state.shape)
+    return back.reshape(state.shape)
 
 
 def solution(mesh):

time: 116 us -> 106 us (0.914)
  Pallas kernels: 105 us -> 96.9 us
    pallas_call x1, Pallas kernels: 51.8 us -> 45.2 us  [per_device(): pl.pallas_call(functools.partial(gather_window, nm, ns), out_shape=(jax.S...]
    another operation x2 -> x0, local copies, waits for them, and re-layouts: 3.93 us -> none  [per_device(): state[:, 0].reshape(rows, nm, patches * cells)]
    reshape x1 -> x2, local copies, waits for them, and re-layouts: 2.4 us -> 5.89 us  [the longest x1 3.47 us: per_device(): flat = state.reshape(rows, nm * patches * cells)]
    pallas_call x1, Pallas kernels: 45.6 us -> 44 us  [per_device(): pl.pallas_call(functools.partial(analyse, cells), out_shape=jax.ShapeDtyp...]
where the time goes in v3:
time: 106 us
  Pallas kernels  96.9 us (91%)
  local copies, waits for them, and re-layouts  6.79 us (6%)
  other arithmetic  2.14 us (2%)
    pallas_call x1, Pallas kernels, per_device(): pl.pallas_call(functools.partial(gather_window, nm, ns), out_shape=(jax.S...  45.2 us
    pallas_call x1, Pallas kernels, per_device(): pl.pallas_call(functools.partial(analyse, cells), out_shape=jax.ShapeDtyp...  44 us
    pallas_call x1, Pallas kernels, per_device(): pl.pallas_call(functools.partial(gram_of_patches, blocks), out_shape=(jax...  7.65 us
    reshape x1, local copies, waits for them, and re-layouts, per_device(): flat = state.reshape(rows, nm * patches * cells)  3.47 us
    reshape x1, local copies, waits for them, and re-layouts, per_device(): return back.reshape(state.shape)  2.42 us

profile of v3, /device:TPU:13, one launch (start us, length us, event | category | flops | bytes accessed | tf_op | source)
XLA Modules:
  0.0 105.9 jit_solution(6410387783465327290)
XLA Ops:
  0.0 0.8 fusion.1
  0.8 1.4 %pad_maximum_fusion.aux_ref = f32[2,4096]{1,0:T(2,128)} fusion(f32[1,4096]{1,0:T(1,128)S(1)} %bitcast.13, f32[1,4096]{1,0:T(1,128)} %bitcast.14), kind=kLoop, calls=%fused_computation | loop fusion | flops 8192 | bytes 65536 | tf_op jit(solution)/shard_map/stack | solution.py:376
  2.1 3.5 %reshape.20.cut_ref = bf16[32,18432]{1,0:T(8,128)(2,1)} reshape(bf16[32,1,32,576]{3,2,1,0:T(8,128)(2,1)} %param.13) | data formatting | bytes 2359296 | tf_op jit(solution)/shard_map/reshape | solution.py:382
  5.6 0.0 copy-start.2
  5.6 0.0 copy-start.3
  5.6 45.2 %gather_window.1 = (bf16[8,32,12288]{2,1,0:T(8,128)(2,1)}, f32[3,2,4096]{2,1,0:T(2,128)}, bf16[8,32,2304]{2,1,0:T(8,128)(2,1)}, bf16[2,32,4096]{2,1,0:T(8,128)(2,1)}) custom-call(bf16[32,4096]{1,0:T(8,128)(2,1)} %yb_ref.1, f32[2,4096]{1,0:T(2,128)} %pad_maximum_fusion.aux_ref, bf16[32,18432]{1,0:T(8,128)(2,1)} %reshape.20.cut_ref), custom_call_target="tpu_custom_call" | custom-call | bytes 41943040 | tf_op jit(solution)/shard_map/gather_window/pallas_call | solution.py:383
  50.9 0.0 copy-done.2
  50.9 0.0 copy-done.3
  50.9 0.0 copy-start.1
  50.9 0.9 copy-done.1
  51.8 0.0 copy-start
  51.8 7.6 %gram_of_patches.1 = (f32[4,256,256]{2,1,0:T(8,128)S(1)}, f32[4,256,1]{2,1,0:T(8,128)S(1)}) custom-call(s32[4,16]{1,0:T(4,128)S(1)} %bitcast.11, f32[4,16]{1,0:T(4,128)S(1)} %bitcast.12, bf16[8,32,12288]{2,1,0:T(8,128)(2,1)} %get-tuple-element.10.win_ref, f32[3,2,4096]{2,1,0:T(2,128)S(1)} %copy-done.1), custom_call_target="tpu_custom_call" | custom-call | flops 2147483648 | bytes 8388608 | tf_op jit(solution)/shard_map/gram_of_patches/pallas_call | solution.py:401
  59.4 0.0 copy-done
  59.5 44.0 %analyse.1 = bf16[32,18432]{1,0:T(8,128)(2,1)S(1)} custom-call(f32[4,256,256]{2,1,0:T(8,128)S(1)} %get-tuple-element.12.system_ref, f32[4,256,1]{2,1,0:T(8,128)S(1)} %get-tuple-element.13.proj_ref, bf16[8,32,2304]{2,1,0:T(8,128)(2,1)S(1)} %copy-done), custom_call_target="tpu_custom_call" | custom-call | flops 8589934592 | bytes 8388608 | tf_op jit(solution)/shard_map/analyse/pallas_call | solution.py:412
  103.5 2.4 %reshape.21 = bf16[32,1,32,576]{3,2,0,1:T(8,128)(2,1)} reshape(bf16[32,18432]{1,0:T(8,128)(2,1)S(1)} %analyse.1) | data formatting | bytes 2359296 | tf_op jit(solution)/shard_map/reshape | solution.py:424
Async XLA Ops:
  5.6 45.3 %copy-start.2 = (s32[4,1,16]{2,1,0:T(1,128)S(1)}, s32[4,1,16]{2,1,0:T(1,128)}, u32[]{:S(2)}) copy-start(s32[4,1,16]{2,1,0:T(1,128)} %param.11) | copy-start | bytes 772
  5.6 45.3 %copy-start.3 = (f32[4,1,16]{2,1,0:T(1,128)S(1)}, f32[4,1,16]{2,1,0:T(1,128)}, u32[]{:S(2)}) copy-start(f32[4,1,16]{2,1,0:T(1,128)} %param.12) | copy-start | bytes 772
  50.9 0.9 copy-start.1
  51.8 7.7 %copy-start = (bf16[8,32,2304]{2,1,0:T(8,128)(2,1)S(1)}, bf16[8,32,2304]{2,1,0:T(8,128)(2,1)}, u32[]{:S(2)}) copy-start(bf16[8,32,2304]{2,1,0:T(8,128)(2,1)} %get-tuple-element.14.col_ref) | copy-start | bytes 3538948
